TPU v7x, 32 devices: a whole 2x2x4 slice. The times are simulated.
32 devices in a mesh: yaw: 4 (over y, x), space: 8 (over z, core).
Axes of the slice: x: 2, y: 2, z: 4, core: 2. Of those that a mesh axis runs over, the one named last changes fastest.
Arguments:
- adjoint: float32 [4, 4, 16, 32, 256], P('yaw', None, 'space'), may hold values from -6 to 6
- viscosity: float32 [4, 16, 32, 256], P('yaw', 'space'), may hold values from 0.25 to 4
- coupling: float32 [4, 4, 4], P('yaw'), may hold values from -3 to 3
- yaw_weight: float32 [4], P('yaw'), may hold values from 0.03 to 0.3
- node_cell: int32 [16384], P('space'), may hold values from 0 to 16383
- node_patch: int32 [16384], P('space'), may hold values from 0 to 2047
- node_normal: float32 [3, 16384], P(None, 'space'), may hold values from -5 to 5
- morph_kernel: float32 [2048, 256], P('space'), may hold values from -0.375 to 0.375
Outputs:
- residual: float32 [4, 4, 16, 32, 256], P('yaw', None, 'space')
- patch_gradient: float32 [3, 2048], P(None, 'space')
- node_gradient: float32 [3, 16384], P(None, 'space')
Inputs may be any that keep to these rules, and one draw needn't show every extreme that they name: node_cell[n] indexes a cell of slab n // 2048, flattened over its 2 x 32 x 256 cells in that order.
All inputs are finite; a program needn't handle non-finite values.
Results may differ from a plain program's by a relative error of at most 0.000098.
Values sent between devices are 32-bit elements; how exact they have to be, the bound alone decides.
A program may use at most 64 MiB of HBM per device.

v0:
```python
import functools

import jax
import jax.numpy as jnp
from jax import lax
from jax.experimental import pallas as pl
from jax.experimental.pallas import tpu as pltpu
from jax.sharding import PartitionSpec as P

LANES = 128
CHUNK = 256
F32 = jnp.float32
BF16 = jnp.bfloat16


def dot(a, b, contract=((1,), (0,))):
    return lax.dot_general(a, b, (contract, ((), ())), preferred_element_type=F32)


def parts(x):
    hi = x.astype(BF16)
    return hi, (x - hi.astype(F32)).astype(BF16)


def each(count, body, first=1):
    if count <= 8:
        for d in range(first, count):
            body(d)
    else:
        lax.fori_loop(first, count, lambda d, c: (body(d), c)[1], 0)


def kernel(
    n_yaw, n_space,
    coup_in, weight_in, adj_in, visc_in, cell_in, patch_in, normal_in, morph_in,
    res, pgrad, ngrad,
    coup, weight, adj, visc, cell, patch, normal, morph,
    before_a, before_v, after_a, after_v,
    pick_row, pick_patch, pick_patch_t, normal8, morph_hi, morph_lo,
    dense, got, grads,
    row_in, load, halo_send, halo_recv, send1, recv1, send3, recv3,
):
    _, fields, layers, ny, nz = adj.shape
    nodes = cell.shape[1]
    owned = morph.shape[1]
    halves = owned // LANES
    used = 3 * halves
    rows = dense.shape[1]
    groups = nz // LANES
    y0, s0 = lax.axis_index("yaw"), lax.axis_index("space")

    def space_peer(d):
        return lax.rem(s0 + d, n_space)

    def yaw_peer(d):
        return lax.rem(y0 + d, n_yaw)

    def everyone(body):
        for dy in reversed(range(n_yaw)):
            each(n_space, functools.partial(body, dy), 0 if dy else 1)

    grads[...] = jnp.zeros_like(grads)
    barrier = pltpu.get_barrier_semaphore()
    each(n_space, lambda d: pl.semaphore_signal(barrier, inc=1, device_id={"space": space_peer(d)}))
    each(n_yaw, lambda d: pl.semaphore_signal(barrier, inc=1, device_id={"yaw": yaw_peer(d)}))
    loads = [
        pltpu.make_async_copy(src, dst, load.at[i])
        for i, (src, dst) in enumerate((
            (adj_in, adj), (visc_in, visc), (coup_in, coup), (cell_in, cell), (patch_in, patch),
            (normal_in, normal), (morph_in, morph), (weight_in, weight),
        ))
    ]
    for copy in loads:
        copy.start()
    pl.semaphore_wait(barrier, n_space + n_yaw - 2)
    each(n_yaw, lambda d: pl.semaphore_signal(row_in, inc=1, device_id={"yaw": yaw_peer(d)}))

    has_before, has_after = s0 > 0, s0 < n_space - 1

    def halo(slot, src, dst, peer):
        return pltpu.make_async_remote_copy(
            src_ref=src, dst_ref=dst, send_sem=halo_send.at[slot], recv_sem=halo_recv.at[slot],
            device_id={"space": peer},
        )

    up = (
        halo(0, adj_in.at[0, :, layers - 1], before_a, s0 + 1),
        halo(1, visc_in.at[0, layers - 1], before_v, s0 + 1),
    )
    down = (
        halo(2, adj_in.at[0, :, 0], after_a, s0 - 1),
        halo(3, visc_in.at[0, 0], after_v, s0 - 1),
    )

    @pl.when(has_after)
    def _():
        for copy in up:
            copy.start()

    @pl.when(has_before)
    def _():
        for copy in down:
            copy.start()

    @pl.when(jnp.logical_not(has_before))
    def _():
        before_a[...] = jnp.zeros_like(before_a)
        before_v[...] = jnp.zeros_like(before_v)

    @pl.when(jnp.logical_not(has_after))
    def _():
        after_a[...] = jnp.zeros_like(after_a)
        after_v[...] = jnp.zeros_like(after_v)

    for copy in loads:
        copy.wait()

    at_y = lax.broadcasted_iota(jnp.int32, (ny, nz), 0)
    at_z = lax.broadcasted_iota(jnp.int32, (ny, nz), 1)
    shifts = (
        (0, 1, at_y > 0), (0, ny - 1, at_y < ny - 1), (1, 1, at_z > 0), (1, nz - 1, at_z < nz - 1)
    )
    for x in range(layers):
        v = visc[0, x]
        total = jnp.zeros_like(v)
        faces = []
        for axis, shift, inside in shifts:
            face = 0.5 * (v + jnp.where(inside, pltpu.roll(v, shift, axis), 0.0))
            total = total + face
            faces.append(jnp.where(inside, face, 0.0))
        inner = {}
        for nb in (x - 1, x + 1):
            if 0 <= nb < layers:
                inner[nb] = 0.5 * (v + visc[0, nb])
                total = total + inner[nb]
        total = total + 2.0
        for f in range(fields):
            a = adj[0, f, x]
            out = total * a
            for g in range(fields):
                out = out + coup[0, f, g] * adj[0, g, x]
            for (axis, shift, _), face in zip(shifts, faces):
                out = out - face * pltpu.roll(a, shift, axis)
            for nb, face in inner.items():
                out = out - face * adj[0, f, nb]
            res[0, f, x] = out

    cells = layers * ny
    for j in range(nodes // CHUNK):
        at = pl.ds(j * CHUNK, CHUNK)
        c = cell[:, at]
        row = (c // LANES) % groups * cells + c // nz
        count = groups * cells
        hot = (lax.broadcasted_iota(jnp.int32, (count, CHUNK), 0) == row).astype(F32).astype(BF16)
        pick_row[0:count, at] = hot
        pick_row[count:2 * count, at] = hot
        low = patch[:, at] % LANES
        hot = (lax.broadcasted_iota(jnp.int32, (LANES, CHUNK), 0) == low).astype(F32)
        pick_patch_t[at, :] = hot.T.astype(BF16)
        pick_patch[0:LANES, at] = hot.astype(BF16)
        pick_patch[LANES:2 * LANES, at] = hot.astype(BF16)
    normal8[...] = jnp.zeros_like(normal8)
    for h in range(halves):
        normal8[3 * h:3 * h + 3, :] = normal[...]
    m_hi, m_lo = parts(morph[...])
    morph_hi[...] = m_hi
    morph_lo[...] = m_lo

    @pl.when(has_before)
    def _():
        for copy in up:
            copy.wait_recv()

    @pl.when(has_after)
    def _():
        for copy in down:
            copy.wait_recv()

    cell_sens = []
    for x in range(layers):
        v = visc[0, x]
        acc = jnp.zeros_like(v)
        for f in range(fields):
            a = adj[0, f, x]
            r = res[0, f, x]
            if x == 0:
                r = r - 0.5 * (v + before_v[...]) * (before_a[f] - a)
            if x == layers - 1:
                r = r - 0.5 * (v + after_v[...]) * (after_a[f] - a)
            res[0, f, x] = r
            acc = acc + a * r
        cell_sens.append(weight[0, 0] * v * acc)
    s = jnp.concatenate(cell_sens, axis=0)
    s = jnp.concatenate([s[:, g * LANES:(g + 1) * LANES] for g in range(groups)], axis=0)
    s = jnp.concatenate(parts(s.T), axis=1)

    owner_rows = n_space * rows
    shape3 = (n_space, rows, CHUNK)
    half_of = lax.broadcasted_iota(jnp.int32, shape3, 0) * halves + lax.broadcasted_iota(jnp.int32, shape3, 1) // 3
    sums_now = jnp.zeros((2 * owner_rows, LANES), F32)
    for j in range(nodes // CHUNK):
        at = pl.ds(j * CHUNK, CHUNK)
        t = dot(s, pick_row[:, at])
        lane = cell[:, at] % LANES
        here = lax.broadcasted_iota(jnp.int32, t.shape, 0) == lane
        sens = jnp.sum(jnp.where(here, t, 0.0), axis=0, keepdims=True)
        part = normal8[:, at] * sens
        high = patch[:, at] // LANES
        spread = jnp.where(half_of == high[None], part[None], 0.0).reshape(owner_rows, CHUNK)
        a = jnp.concatenate(parts(spread), axis=0)
        sums_now = sums_now + dot(a, pick_patch_t[at, :])
    dense[...] = (sums_now[:owner_rows] + sums_now[owner_rows:]).reshape(dense.shape)

    def site(q, d):
        owner = space_peer(d)
        return 2 * q + lax.rem(owner, 2), owner

    is_site = lax.rem(y0, 2) == lax.rem(s0, 2)
    pair = lax.div(y0, 2)
    pairs = n_yaw // 2

    def to_site(dq, d):
        yaw, owner = site(lax.rem(pair + dq, pairs), d)
        return pltpu.make_async_remote_copy(
            src_ref=dense.at[owner, 0:used], dst_ref=got.at[y0, s0, 0:used],
            send_sem=send1.at[dq, d], recv_sem=recv1.at[y0, s0], device_id={"yaw": yaw, "space": owner},
        )

    def from_slab(dy, d):
        return pltpu.make_async_remote_copy(
            src_ref=dense.at[space_peer(d), 0:used], dst_ref=got.at[yaw_peer(dy), space_peer(d), 0:used],
            send_sem=send1.at[0, d], recv_sem=recv1.at[yaw_peer(dy), space_peer(d)],
            device_id={"yaw": yaw_peer(dy), "space": space_peer(d)},
        )

    def sites(act):
        for dq in reversed(range(pairs)):
            each(n_space, lambda d: act(to_site(dq, d)), 0 if dq else 1)

        @pl.when(jnp.logical_not(is_site))
        def _():
            act(to_site(0, 0))

    pl.semaphore_wait(row_in, n_yaw - 1)
    sites(lambda copy: copy.start())

    def to_slab(dy, d):
        return pltpu.make_async_remote_copy(
            src_ref=grads.at[s0, 0:used], dst_ref=grads.at[s0, 0:used],
            send_sem=send3.at[dy, d], recv_sem=recv3.at[s0],
            device_id={"yaw": 2 * pair + lax.rem(y0 + dy, 2), "space": space_peer(d)},
        )

    def slabs(act):
        for dy in (1, 0):
            each(n_space, lambda d: act(to_slab(dy, d)), 0 if dy else 1)

    def from_owner(d):
        yaw, owner = site(pair, d)
        return pltpu.make_async_remote_copy(
            src_ref=grads.at[owner, 0:used], dst_ref=grads.at[owner, 0:used],
            send_sem=send3.at[0, d], recv_sem=recv3.at[owner], device_id={"yaw": yaw, "space": owner},
        )

    @pl.when(is_site)
    def _():
        got[y0, s0] = dense[s0]
        everyone(lambda dy, d: from_slab(dy, d).wait_recv())
        p = jnp.sum(jnp.sum(got[...], axis=0), axis=0)
        p = jnp.concatenate([p[3 * h:3 * h + 3] for h in range(halves)], axis=1)
        p = jnp.concatenate([p, jnp.zeros((5, owned), F32)], axis=0)
        hi, lo = parts(p)
        both = jnp.concatenate([hi.astype(F32), lo.astype(F32)], axis=0).astype(BF16)
        smooth = dot(both, morph_hi[...], ((1,), (1,))) + dot(both, morph_lo[...], ((1,), (1,)))
        g = p + smooth[0:8] + smooth[8:16]
        for h in range(halves):
            grads[s0, 3 * h:3 * h + 3] = g[0:3, h * LANES:(h + 1) * LANES]
        slabs(lambda copy: copy.start())

    @pl.when(jnp.logical_not(is_site))
    def _():
        from_owner(0).wait_recv()

    each(n_space, lambda d: from_owner(d).wait_recv())
    for h in range(halves):
        pgrad[:, h * LANES:(h + 1) * LANES] = grads[s0, 3 * h:3 * h + 3]
    allg = jnp.concatenate(parts(grads[...].reshape(owner_rows, LANES)), axis=1)
    for j in range(nodes // CHUNK):
        at = pl.ds(j * CHUNK, CHUNK)
        e = dot(allg, pick_patch[:, at]).reshape(shape3)
        high = patch[:, at] // LANES
        e = jnp.sum(jnp.where(half_of == high[None], e, 0.0), axis=0)
        out = e[0:3]
        for h in range(1, halves):
            out = out + e[3 * h:3 * h + 3]
        ngrad[:, at] = out

    @pl.when(has_before)
    def _():
        for copy in down:
            copy.wait_send()

    @pl.when(has_after)
    def _():
        for copy in up:
            copy.wait_send()

    sites(lambda copy: copy.wait_send())

    @pl.when(is_site)
    def _():
        slabs(lambda copy: copy.wait_send())


def write(*refs):
    srcs, dsts, sem = refs[:3], refs[3:6], refs[6]
    copies = [pltpu.make_async_copy(s, d, sem.at[i]) for i, (s, d) in enumerate(zip(srcs, dsts))]
    for copy in copies:
        copy.start()
    for copy in copies:
        copy.wait()


def shards(
    n_yaw, n_space,
    adjoint, viscosity, coupling, yaw_weight, node_cell, node_patch, node_normal, morph_kernel,
):
    _, fields, layers, ny, nz = adjoint.shape
    nodes = node_cell.shape[0]
    owned = morph_kernel.shape[1]
    rows = -(-3 * (owned // LANES) // 8) * 8
    vmem = pl.BlockSpec(memory_space=pltpu.VMEM)
    anywhere = pl.BlockSpec(memory_space=pl.ANY)
    dma = pltpu.SemaphoreType.DMA
    outs = pl.pallas_call(
        functools.partial(kernel, n_yaw, n_space),
        out_shape=(
            pltpu.VMEM(adjoint.shape, F32),
            pltpu.VMEM((3, owned), F32),
            pltpu.VMEM((3, nodes), F32),
        ),
        in_specs=[pl.BlockSpec(memory_space=pltpu.HBM)] * 8,
        out_specs=(vmem, vmem, vmem),
        scratch_shapes=[
            pltpu.SMEM(coupling.shape, F32),
            pltpu.SMEM((1, 1), F32),
            pltpu.VMEM(adjoint.shape, F32),
            pltpu.VMEM(viscosity.shape, F32),
            pltpu.VMEM((1, nodes), jnp.int32),
            pltpu.VMEM((1, nodes), jnp.int32),
            pltpu.VMEM(node_normal.shape, F32),
            pltpu.VMEM(morph_kernel.shape, F32),
            pltpu.VMEM((fields, ny, nz), F32),
            pltpu.VMEM((ny, nz), F32),
            pltpu.VMEM((fields, ny, nz), F32),
            pltpu.VMEM((ny, nz), F32),
            pltpu.VMEM((2 * layers * ny * nz // LANES, nodes), BF16),
            pltpu.VMEM((2 * LANES, nodes), BF16),
            pltpu.VMEM((nodes, LANES), BF16),
            pltpu.VMEM((rows, nodes), F32),
            pltpu.VMEM((owned, owned), BF16),
            pltpu.VMEM((owned, owned), BF16),
            pltpu.VMEM((n_space, rows, LANES), F32),
            pltpu.VMEM((n_yaw, n_space, rows, LANES), F32),
            pltpu.VMEM((n_space, rows, LANES), F32),
            pltpu.SemaphoreType.REGULAR,
            dma((8,)), dma((4,)), dma((4,)),
            dma((n_yaw // 2, n_space)), dma((n_yaw, n_space)),
            dma((2, n_space)), dma((n_space,)),
        ],
        compiler_params=pltpu.CompilerParams(
            collective_id=0, has_side_effects=True, vmem_limit_bytes=56 * 1024 * 1024
        ),
        cost_estimate=pl.CostEstimate(flops=400_000_000, bytes_accessed=1_000_000, transcendentals=0),
    )(
        coupling, yaw_weight[None], adjoint, viscosity,
        node_cell[None], node_patch[None], node_normal, morph_kernel,
    )
    return pl.pallas_call(
        write,
        out_shape=tuple(jax.ShapeDtypeStruct(o.shape, F32) for o in outs),
        in_specs=[vmem] * 3,
        out_specs=(anywhere,) * 3,
        scratch_shapes=[dma((3,))],
        compiler_params=pltpu.CompilerParams(vmem_limit_bytes=2 * 1024 * 1024),
    )(*outs)


def solution(mesh):
    return jax.shard_map(
        functools.partial(shards, mesh.shape["yaw"], mesh.shape["space"]),
        mesh=mesh,
        in_specs=(
            P("yaw", None, "space", None, None),
            P("yaw", "space", None, None),
            P("yaw", None, None),
            P("yaw"),
            P("space"),
            P("space"),
            P(None, "space"),
            P("space", None),
        ),
        out_specs=(P("yaw", None, "space", None, None), P(None, "space"), P(None, "space")),
        check_vma=False,
    )
```

profile of v0, /device:TPU:0, one launch (start us, length us, event | category | flops | bytes accessed | tf_op | source)
XLA Modules:
  0.0 22.0 jit_solution(14722393251232575167)
XLA Ops:
  1.3 20.0 %shard_map.103 = (f32[1,4,2,32,256]{4,3,2,1,0:T(8,128)S(1)}, f32[3,256]{1,0:T(4,128)S(1)}, f32[3,2048]{1,0:T(4,128)S(1)}) custom-call(f32[1,4,4]{2,1,0:T(4,128)} %coup_in.1, f32[1,1]{1,0:T(1,128)} %bitcast.3.weight_in, f32[1,4,2,32,256]{4,3,2,1,0:T(8,128)} %adj_in.1, f32[1,2,32,256]{3,2,1,0:T(8,128)} %visc_in.1, s32[1,2048]{1,0:T(1,128)} %bitcast.4, ...), custom_call_target="tpu_custom_call" | custom-call | flops 400000000 | bytes 1000000 | tf_op jit(solution)/shard_map/pallas_call | solution.py:335
  21.3 0.7 %shard_map.104 = (f32[1,4,2,32,256]{4,3,2,1,0:T(8,128)}, f32[3,256]{1,0:T(4,128)}, f32[3,2048]{1,0:T(4,128)}) custom-call(f32[1,4,2,32,256]{4,3,2,1,0:T(8,128)S(1)} %get-tuple-element.6.refs_0_, f32[3,256]{1,0:T(4,128)S(1)} %get-tuple-element.7.refs_1_, f32[3,2048]{1,0:T(4,128)S(1)} %get-tuple-element.8.refs_2_), custom_call_target="tpu_custom_call" | custom-call | tf_op jit(solution)/shard_map/pallas_call | solution.py:379
where the time goes:
time: 22.2 us; the launch traced here: 22 us
  Pallas kernels  20.7 us (93%)
  between operations  1.29 us (6%)
    pallas_call x1, Pallas kernels, shards(): pl.pallas_call(functools.partial(kernel, n_yaw, n_space), out_shape=(pltp...  20 us
    pallas_call x1, Pallas kernels, shards(): pl.pallas_call(write, out_shape=tuple((jax.ShapeDtypeStruct(o.shape, F32)...  0.74 us

commit v1 on v0

--- a/solution.py
+++ b/solution.py
@@ -33,12 +33,12 @@
 def kernel(
     n_yaw, n_space,
     coup_in, weight_in, adj_in, visc_in, cell_in, patch_in, normal_in, morph_in,
-    res, pgrad, ngrad,
-    coup, weight, adj, visc, cell, patch, normal, morph,
+    res, pgrad, grads_out, patch, pick_patch,
+    coup, weight, adj, visc, cell, normal, morph,
     before_a, before_v, after_a, after_v,
-    pick_row, pick_patch, pick_patch_t, normal8, morph_hi, morph_lo,
+    pick_row, pick_patch_t, normal8, morph_hi, morph_lo,
     dense, got, grads,
-    row_in, load, halo_send, halo_recv, send1, recv1, send3, recv3,
+    row_in, load, halo_send, halo_recv, send1, recv1, send3, recv3, morph_send, morph_recv,
 ):
     _, fields, layers, ny, nz = adj.shape
     nodes = cell.shape[1]
@@ -55,27 +55,49 @@
     def yaw_peer(d):
         return lax.rem(y0 + d, n_yaw)
 
-    def everyone(body):
-        for dy in reversed(range(n_yaw)):
-            each(n_space, functools.partial(body, dy), 0 if dy else 1)
-
-    grads[...] = jnp.zeros_like(grads)
+    has_before, has_after = s0 > 0, s0 < n_space - 1
+
+    def enter(d):
+        pl.semaphore_signal(barrier, inc=1, device_id={"space": space_peer(d)})
+
     barrier = pltpu.get_barrier_semaphore()
-    each(n_space, lambda d: pl.semaphore_signal(barrier, inc=1, device_id={"space": space_peer(d)}))
-    each(n_yaw, lambda d: pl.semaphore_signal(barrier, inc=1, device_id={"yaw": yaw_peer(d)}))
+    enter(n_space - 1)
+    if n_space > 2:
+        enter(1)
     loads = [
         pltpu.make_async_copy(src, dst, load.at[i])
         for i, (src, dst) in enumerate((
             (adj_in, adj), (visc_in, visc), (coup_in, coup), (cell_in, cell), (patch_in, patch),
-            (normal_in, normal), (morph_in, morph), (weight_in, weight),
+            (normal_in, normal), (weight_in, weight),
         ))
     ]
-    for copy in loads:
+    for copy in loads[:2]:
         copy.start()
+    each(n_space - 1, enter, 2)
+    each(n_yaw, lambda d: pl.semaphore_signal(barrier, inc=1, device_id={"yaw": yaw_peer(d)}))
+    for copy in loads[2:]:
+        copy.start()
+    grads[...] = jnp.zeros_like(grads)
+
+    core = lax.rem(s0, 2)
+    first = s0 - core
+    turn = lax.rem(y0, 2)
+    mine = first + turn
+    is_site = core == 1
+    own_morph = pltpu.make_async_copy(morph_in, morph, load.at[7])
+    near_morph = pltpu.make_async_remote_copy(
+        src_ref=morph_in, dst_ref=morph, send_sem=morph_send, recv_sem=morph_recv,
+        device_id={"space": first + 1},
+    )
+    uses_own = jnp.logical_and(is_site, turn == 1)
+    gets_near = jnp.logical_and(is_site, turn == 0)
+    gives_near = jnp.logical_and(core == 0, turn == 0)
+
+    @pl.when(uses_own)
+    def _():
+        own_morph.start()
+
     pl.semaphore_wait(barrier, n_space + n_yaw - 2)
-    each(n_yaw, lambda d: pl.semaphore_signal(row_in, inc=1, device_id={"yaw": yaw_peer(d)}))
-
-    has_before, has_after = s0 > 0, s0 < n_space - 1
 
     def halo(slot, src, dst, peer):
         return pltpu.make_async_remote_copy(
@@ -84,23 +106,32 @@
         )
 
     up = (
-        halo(0, adj_in.at[0, :, layers - 1], before_a, s0 + 1),
-        halo(1, visc_in.at[0, layers - 1], before_v, s0 + 1),
+        halo(0, adj.at[0, :, layers - 1], before_a, s0 + 1),
+        halo(1, visc.at[0, layers - 1], before_v, s0 + 1),
     )
     down = (
         halo(2, adj_in.at[0, :, 0], after_a, s0 - 1),
         halo(3, visc_in.at[0, 0], after_v, s0 - 1),
     )
 
+    @pl.when(has_before)
+    def _():
+        for copy in down:
+            copy.start()
+
+    for copy in loads[:2]:
+        copy.wait()
+
     @pl.when(has_after)
     def _():
         for copy in up:
             copy.start()
 
-    @pl.when(has_before)
-    def _():
-        for copy in down:
-            copy.start()
+    each(n_yaw, lambda d: pl.semaphore_signal(row_in, inc=1, device_id={"yaw": yaw_peer(d)}))
+
+    @pl.when(gives_near)
+    def _():
+        near_morph.start()
 
     @pl.when(jnp.logical_not(has_before))
     def _():
@@ -112,7 +143,7 @@
         after_a[...] = jnp.zeros_like(after_a)
         after_v[...] = jnp.zeros_like(after_v)
 
-    for copy in loads:
+    for copy in loads[2:]:
         copy.wait()
 
     at_y = lax.broadcasted_iota(jnp.int32, (ny, nz), 0)
@@ -162,9 +193,20 @@
     normal8[...] = jnp.zeros_like(normal8)
     for h in range(halves):
         normal8[3 * h:3 * h + 3, :] = normal[...]
-    m_hi, m_lo = parts(morph[...])
-    morph_hi[...] = m_hi
-    morph_lo[...] = m_lo
+
+    @pl.when(uses_own)
+    def _():
+        own_morph.wait()
+
+    @pl.when(gets_near)
+    def _():
+        near_morph.wait_recv()
+
+    @pl.when(is_site)
+    def _():
+        m_hi, m_lo = parts(morph[...])
+        morph_hi[...] = m_hi
+        morph_lo[...] = m_lo
 
     @pl.when(has_before)
     def _():
@@ -189,7 +231,7 @@
                 r = r - 0.5 * (v + after_v[...]) * (after_a[f] - a)
             res[0, f, x] = r
             acc = acc + a * r
-        cell_sens.append(weight[0, 0] * v * acc)
+        cell_sens.append(weight[0] * v * acc)
     s = jnp.concatenate(cell_sens, axis=0)
     s = jnp.concatenate([s[:, g * LANES:(g + 1) * LANES] for g in range(groups)], axis=0)
     s = jnp.concatenate(parts(s.T), axis=1)
@@ -211,61 +253,66 @@
         sums_now = sums_now + dot(a, pick_patch_t[at, :])
     dense[...] = (sums_now[:owner_rows] + sums_now[owner_rows:]).reshape(dense.shape)
 
-    def site(q, d):
-        owner = space_peer(d)
-        return 2 * q + lax.rem(owner, 2), owner
-
-    is_site = lax.rem(y0, 2) == lax.rem(s0, 2)
     pair = lax.div(y0, 2)
-    pairs = n_yaw // 2
-
-    def to_site(dq, d):
-        yaw, owner = site(lax.rem(pair + dq, pairs), d)
+
+    def owner_of(d):
+        return lax.rem(mine + d, n_space)
+
+    def to_site(q, d):
+        owner = owner_of(d)
+        odd = lax.rem(owner, 2)
         return pltpu.make_async_remote_copy(
             src_ref=dense.at[owner, 0:used], dst_ref=got.at[y0, s0, 0:used],
-            send_sem=send1.at[dq, d], recv_sem=recv1.at[y0, s0], device_id={"yaw": yaw, "space": owner},
+            send_sem=send1.at[q, d], recv_sem=recv1.at[y0, s0],
+            device_id={"yaw": 2 * q + odd, "space": owner - odd + 1},
         )
 
-    def from_slab(dy, d):
+    def from_slab(yaw, slab):
         return pltpu.make_async_remote_copy(
-            src_ref=dense.at[space_peer(d), 0:used], dst_ref=got.at[yaw_peer(dy), space_peer(d), 0:used],
-            send_sem=send1.at[0, d], recv_sem=recv1.at[yaw_peer(dy), space_peer(d)],
-            device_id={"yaw": yaw_peer(dy), "space": space_peer(d)},
+            src_ref=dense.at[0, 0:used], dst_ref=got.at[yaw, slab, 0:used],
+            send_sem=send1.at[0, 0], recv_sem=recv1.at[yaw, slab], device_id={"yaw": yaw, "space": slab},
         )
 
     def sites(act):
-        for dq in reversed(range(pairs)):
-            each(n_space, lambda d: act(to_site(dq, d)), 0 if dq else 1)
-
-        @pl.when(jnp.logical_not(is_site))
-        def _():
-            act(to_site(0, 0))
+        for q in range(n_yaw // 2):
+            @pl.when(jnp.logical_not(jnp.logical_and(is_site, pair == q)))
+            def _():
+                act(to_site(q, 0))
+
+            each(n_space, lambda d: act(to_site(q, d)))
 
     pl.semaphore_wait(row_in, n_yaw - 1)
     sites(lambda copy: copy.start())
 
-    def to_slab(dy, d):
+    def to_slab(k, slab):
         return pltpu.make_async_remote_copy(
-            src_ref=grads.at[s0, 0:used], dst_ref=grads.at[s0, 0:used],
-            send_sem=send3.at[dy, d], recv_sem=recv3.at[s0],
-            device_id={"yaw": 2 * pair + lax.rem(y0 + dy, 2), "space": space_peer(d)},
+            src_ref=grads.at[mine, 0:used], dst_ref=grads.at[mine, 0:used],
+            send_sem=send3.at[k, slab], recv_sem=recv3.at[mine],
+            device_id={"yaw": 2 * pair + k, "space": slab},
         )
 
     def slabs(act):
-        for dy in (1, 0):
-            each(n_space, lambda d: act(to_slab(dy, d)), 0 if dy else 1)
+        def one(slab):
+            for k in range(2):
+                @pl.when(jnp.logical_not(jnp.logical_and(slab == s0, turn == k)))
+                def _():
+                    act(to_slab(k, slab))
+
+        each(n_space, one, 0)
 
     def from_owner(d):
-        yaw, owner = site(pair, d)
+        owner = owner_of(d)
         return pltpu.make_async_remote_copy(
             src_ref=grads.at[owner, 0:used], dst_ref=grads.at[owner, 0:used],
-            send_sem=send3.at[0, d], recv_sem=recv3.at[owner], device_id={"yaw": yaw, "space": owner},
+            send_sem=send3.at[0, 0], recv_sem=recv3.at[owner],
+            device_id={"yaw": 2 * pair + lax.rem(owner, 2), "space": owner - lax.rem(owner, 2) + 1},
         )
 
     @pl.when(is_site)
     def _():
-        got[y0, s0] = dense[s0]
-        everyone(lambda dy, d: from_slab(dy, d).wait_recv())
+        got[y0, s0] = dense[mine]
+        for dy in reversed(range(n_yaw)):
+            each(n_space, lambda d: from_slab(yaw_peer(dy), space_peer(d)).wait_recv(), 0 if dy else 1)
         p = jnp.sum(jnp.sum(got[...], axis=0), axis=0)
         p = jnp.concatenate([p[3 * h:3 * h + 3] for h in range(halves)], axis=1)
         p = jnp.concatenate([p, jnp.zeros((5, owned), F32)], axis=0)
@@ -274,7 +321,7 @@
         smooth = dot(both, morph_hi[...], ((1,), (1,))) + dot(both, morph_lo[...], ((1,), (1,)))
         g = p + smooth[0:8] + smooth[8:16]
         for h in range(halves):
-            grads[s0, 3 * h:3 * h + 3] = g[0:3, h * LANES:(h + 1) * LANES]
+            grads[mine, 3 * h:3 * h + 3] = g[0:3, h * LANES:(h + 1) * LANES]
         slabs(lambda copy: copy.start())
 
     @pl.when(jnp.logical_not(is_site))
@@ -284,7 +331,42 @@
     each(n_space, lambda d: from_owner(d).wait_recv())
     for h in range(halves):
         pgrad[:, h * LANES:(h + 1) * LANES] = grads[s0, 3 * h:3 * h + 3]
-    allg = jnp.concatenate(parts(grads[...].reshape(owner_rows, LANES)), axis=1)
+    grads_out[...] = grads[...]
+
+    @pl.when(has_before)
+    def _():
+        for copy in down:
+            copy.wait_send()
+
+    @pl.when(has_after)
+    def _():
+        for copy in up:
+            copy.wait_send()
+
+    @pl.when(gives_near)
+    def _():
+        near_morph.wait_send()
+
+    sites(lambda copy: copy.wait_send())
+
+    @pl.when(is_site)
+    def _():
+        slabs(lambda copy: copy.wait_send())
+
+
+def finish(res, pgrad, grads, patch, pick_patch, res_out, pgrad_out, ngrad_out, ngrad, sem):
+    n_space, rows, _ = grads.shape
+    nodes = patch.shape[1]
+    halves = pgrad.shape[1] // LANES
+    copies = [
+        pltpu.make_async_copy(src, dst, sem.at[i])
+        for i, (src, dst) in enumerate(((res, res_out), (pgrad, pgrad_out), (ngrad, ngrad_out)))
+    ]
+    for copy in copies[:2]:
+        copy.start()
+    shape3 = (n_space, rows, CHUNK)
+    half_of = lax.broadcasted_iota(jnp.int32, shape3, 0) * halves + lax.broadcasted_iota(jnp.int32, shape3, 1) // 3
+    allg = jnp.concatenate(parts(grads[...].reshape(n_space * rows, LANES)), axis=1)
     for j in range(nodes // CHUNK):
         at = pl.ds(j * CHUNK, CHUNK)
         e = dot(allg, pick_patch[:, at]).reshape(shape3)
@@ -294,29 +376,7 @@
         for h in range(1, halves):
             out = out + e[3 * h:3 * h + 3]
         ngrad[:, at] = out
-
-    @pl.when(has_before)
-    def _():
-        for copy in down:
-            copy.wait_send()
-
-    @pl.when(has_after)
-    def _():
-        for copy in up:
-            copy.wait_send()
-
-    sites(lambda copy: copy.wait_send())
-
-    @pl.when(is_site)
-    def _():
-        slabs(lambda copy: copy.wait_send())
-
-
-def write(*refs):
-    srcs, dsts, sem = refs[:3], refs[3:6], refs[6]
-    copies = [pltpu.make_async_copy(s, d, sem.at[i]) for i, (s, d) in enumerate(zip(srcs, dsts))]
-    for copy in copies:
-        copy.start()
+    copies[2].start()
     for copy in copies:
         copy.wait()
 
@@ -337,16 +397,17 @@
         out_shape=(
             pltpu.VMEM(adjoint.shape, F32),
             pltpu.VMEM((3, owned), F32),
-            pltpu.VMEM((3, nodes), F32),
+            pltpu.VMEM((n_space, rows, LANES), F32),
+            pltpu.VMEM((1, nodes), jnp.int32),
+            pltpu.VMEM((2 * LANES, nodes), BF16),
         ),
         in_specs=[pl.BlockSpec(memory_space=pltpu.HBM)] * 8,
-        out_specs=(vmem, vmem, vmem),
+        out_specs=(vmem,) * 5,
         scratch_shapes=[
             pltpu.SMEM(coupling.shape, F32),
-            pltpu.SMEM((1, 1), F32),
+            pltpu.SMEM((1,), F32),
             pltpu.VMEM(adjoint.shape, F32),
             pltpu.VMEM(viscosity.shape, F32),
-            pltpu.VMEM((1, nodes), jnp.int32),
             pltpu.VMEM((1, nodes), jnp.int32),
             pltpu.VMEM(node_normal.shape, F32),
             pltpu.VMEM(morph_kernel.shape, F32),
@@ -355,7 +416,6 @@
             pltpu.VMEM((fields, ny, nz), F32),
             pltpu.VMEM((ny, nz), F32),
             pltpu.VMEM((2 * layers * ny * nz // LANES, nodes), BF16),
-            pltpu.VMEM((2 * LANES, nodes), BF16),
             pltpu.VMEM((nodes, LANES), BF16),
             pltpu.VMEM((rows, nodes), F32),
             pltpu.VMEM((owned, owned), BF16),
@@ -366,23 +426,27 @@
             pltpu.SemaphoreType.REGULAR,
             dma((8,)), dma((4,)), dma((4,)),
             dma((n_yaw // 2, n_space)), dma((n_yaw, n_space)),
-            dma((2, n_space)), dma((n_space,)),
+            dma((2, n_space)), dma((n_space,)), dma, dma,
         ],
         compiler_params=pltpu.CompilerParams(
             collective_id=0, has_side_effects=True, vmem_limit_bytes=56 * 1024 * 1024
         ),
         cost_estimate=pl.CostEstimate(flops=400_000_000, bytes_accessed=1_000_000, transcendentals=0),
     )(
-        coupling, yaw_weight[None], adjoint, viscosity,
+        coupling, yaw_weight, adjoint, viscosity,
         node_cell[None], node_patch[None], node_normal, morph_kernel,
     )
     return pl.pallas_call(
-        write,
-        out_shape=tuple(jax.ShapeDtypeStruct(o.shape, F32) for o in outs),
-        in_specs=[vmem] * 3,
+        finish,
+        out_shape=(
+            jax.ShapeDtypeStruct(adjoint.shape, F32),
+            jax.ShapeDtypeStruct((3, owned), F32),
+            jax.ShapeDtypeStruct((3, nodes), F32),
+        ),
+        in_specs=[vmem] * 5,
         out_specs=(anywhere,) * 3,
-        scratch_shapes=[dma((3,))],
-        compiler_params=pltpu.CompilerParams(vmem_limit_bytes=2 * 1024 * 1024),
+        scratch_shapes=[pltpu.VMEM((3, nodes), F32), dma((3,))],
+        compiler_params=pltpu.CompilerParams(vmem_limit_bytes=4 * 1024 * 1024),
     )(*outs)
 
 

time: 22.2 us -> 21.1 us (0.950)
  Pallas kernels: 20.7 us -> 19.6 us
    pallas_call x1, Pallas kernels: 20 us -> 18.7 us  [shards(): pl.pallas_call(functools.partial(kernel, n_yaw, n_space), out_shape=(pltp...]
where the time goes in v1:
time: 21.1 us; the launch traced here: 20.9 us
  Pallas kernels  19.6 us (93%)
  between operations  1.29 us (6%)
    pallas_call x1, Pallas kernels, shards(): pl.pallas_call(functools.partial(kernel, n_yaw, n_space), out_shape=(pltp...  18.7 us
    pallas_call x1, Pallas kernels, shards(): pl.pallas_call(finish, out_shape=(jax.ShapeDtypeStruct(adjoint.shape, F32...  0.95 us

profile of v1, /device:TPU:0, one launch (start us, length us, event | category | flops | bytes accessed | tf_op | source)
XLA Modules:
  0.0 20.9 jit_solution(14423881471881896852)
XLA Ops:
  1.3 18.7 %shard_map.103 = (f32[1,4,2,32,256]{4,3,2,1,0:T(8,128)S(1)}, f32[3,256]{1,0:T(4,128)S(1)}, f32[8,8,128]{2,1,0:T(8,128)S(1)}, s32[1,2048]{1,0:T(1,128)S(1)}, bf16[256,2048]{1,0:T(8,128)(2,1)S(1)}) custom-call(f32[1,4,4]{2,1,0:T(4,128)} %coup_in.1, f32[1]{0:T(128)S(6)} %copy.11.weight_in, f32[1,4,2,32,256]{4,3,2,1,0:T(8,128)} %adj_in.1, ...), custom_call_target="tpu_custom_call" | custom-call | flops 400000000 | bytes 1000000 | tf_op jit(solution)/shard_map/pallas_call | solution.py:395
  20.0 1.0 %shard_map.104 = (f32[1,4,2,32,256]{4,3,2,1,0:T(8,128)}, f32[3,256]{1,0:T(4,128)}, f32[3,2048]{1,0:T(4,128)}) custom-call(f32[1,4,2,32,256]{4,3,2,1,0:T(8,128)S(1)} %get-tuple-element.8.res, f32[3,256]{1,0:T(4,128)S(1)} %get-tuple-element.9.pgrad, f32[8,8,128]{2,1,0:T(8,128)S(1)} %get-tuple-element.10.grads, s32[1,2048]{1,0:T(1,128)S(1)} %get-tuple-element.11.patch, ...), custom_call_target="tpu_custom_call" | custom-call | tf_op jit(solution)/shard_map/pallas_call | solution.py:439

commit v2 on v1

--- a/solution.py
+++ b/solution.py
@@ -38,7 +38,7 @@
     before_a, before_v, after_a, after_v,
     pick_row, pick_patch_t, normal8, morph_hi, morph_lo,
     dense, got, grads,
-    row_in, load, halo_send, halo_recv, send1, recv1, send3, recv3, morph_send, morph_recv,
+    above_in, row_in, load, halo_send, halo_recv, send1, recv1, send3, recv3, morph_send, morph_recv,
 ):
     _, fields, layers, ny, nz = adj.shape
     nodes = cell.shape[1]
@@ -57,13 +57,13 @@
 
     has_before, has_after = s0 > 0, s0 < n_space - 1
 
-    def enter(d):
-        pl.semaphore_signal(barrier, inc=1, device_id={"space": space_peer(d)})
-
     barrier = pltpu.get_barrier_semaphore()
-    enter(n_space - 1)
-    if n_space > 2:
-        enter(1)
+
+    def enter(slab):
+        pl.semaphore_signal(barrier, inc=1, device_id={"space": slab})
+
+    pl.when(has_before)(lambda: enter(s0 - 1))
+    pl.when(has_after)(lambda: enter(s0 + 1))
     loads = [
         pltpu.make_async_copy(src, dst, load.at[i])
         for i, (src, dst) in enumerate((
@@ -73,8 +73,8 @@
     ]
     for copy in loads[:2]:
         copy.start()
-    each(n_space - 1, enter, 2)
     each(n_yaw, lambda d: pl.semaphore_signal(barrier, inc=1, device_id={"yaw": yaw_peer(d)}))
+    each(n_space, lambda slab: pl.when(slab > s0 + 1)(lambda: enter(slab)), 2)
     for copy in loads[2:]:
         copy.start()
     grads[...] = jnp.zeros_like(grads)
@@ -97,7 +97,7 @@
     def _():
         own_morph.start()
 
-    pl.semaphore_wait(barrier, n_space + n_yaw - 2)
+    pl.semaphore_wait(barrier, s0 + has_after.astype(jnp.int32) + n_yaw - 1)
 
     def halo(slot, src, dst, peer):
         return pltpu.make_async_remote_copy(
@@ -127,7 +127,9 @@
         for copy in up:
             copy.start()
 
-    each(n_yaw, lambda d: pl.semaphore_signal(row_in, inc=1, device_id={"yaw": yaw_peer(d)}))
+    each(n_space - 2, lambda slab: pl.when(slab < s0 - 1)(
+        lambda: pl.semaphore_signal(above_in, inc=1, device_id={"space": slab})
+    ), 0)
 
     @pl.when(gives_near)
     def _():
@@ -207,6 +209,12 @@
         m_hi, m_lo = parts(morph[...])
         morph_hi[...] = m_hi
         morph_lo[...] = m_lo
+
+    @pl.when(s0 < n_space - 2)
+    def _():
+        pl.semaphore_wait(above_in, n_space - 2 - s0)
+
+    each(n_yaw, lambda d: pl.semaphore_signal(row_in, inc=1, device_id={"yaw": yaw_peer(d)}))
 
     @pl.when(has_before)
     def _():
@@ -423,7 +431,7 @@
             pltpu.VMEM((n_space, rows, LANES), F32),
             pltpu.VMEM((n_yaw, n_space, rows, LANES), F32),
             pltpu.VMEM((n_space, rows, LANES), F32),
-            pltpu.SemaphoreType.REGULAR,
+            pltpu.SemaphoreType.REGULAR, pltpu.SemaphoreType.REGULAR,
             dma((8,)), dma((4,)), dma((4,)),
             dma((n_yaw // 2, n_space)), dma((n_yaw, n_space)),
             dma((2, n_space)), dma((n_space,)), dma, dma,

time: 21.1 us -> 20 us (0.948)
  Pallas kernels: 19.6 us -> 18.5 us
    pallas_call x1, Pallas kernels: 18.7 us -> 17.6 us  [shards(): pl.pallas_call(functools.partial(kernel, n_yaw, n_space), out_shape=(pltp...]
where the time goes in v2:
time: 20 us; the launch traced here: 19.8 us
  Pallas kernels  18.5 us (92%)
  between operations  1.29 us (6%)
    pallas_call x1, Pallas kernels, shards(): pl.pallas_call(functools.partial(kernel, n_yaw, n_space), out_shape=(pltp...  17.6 us
    pallas_call x1, Pallas kernels, shards(): pl.pallas_call(finish, out_shape=(jax.ShapeDtypeStruct(adjoint.shape, F32...  0.95 us

profile of v2, /device:TPU:0, one launch (start us, length us, event | category | flops | bytes accessed | tf_op | source)
XLA Modules:
  0.0 19.8 jit_solution(5273722057427619206)
XLA Ops:
  1.3 17.6 %shard_map.103 = (f32[1,4,2,32,256]{4,3,2,1,0:T(8,128)S(1)}, f32[3,256]{1,0:T(4,128)S(1)}, f32[8,8,128]{2,1,0:T(8,128)S(1)}, s32[1,2048]{1,0:T(1,128)S(1)}, bf16[256,2048]{1,0:T(8,128)(2,1)S(1)}) custom-call(f32[1,4,4]{2,1,0:T(4,128)} %coup_in.1, f32[1]{0:T(128)S(6)} %copy.11.weight_in, f32[1,4,2,32,256]{4,3,2,1,0:T(8,128)} %adj_in.1, ...), custom_call_target="tpu_custom_call" | custom-call | flops 400000000 | bytes 1000000 | tf_op jit(solution)/shard_map/pallas_call | solution.py:403
  18.9 0.9 %shard_map.104 = (f32[1,4,2,32,256]{4,3,2,1,0:T(8,128)}, f32[3,256]{1,0:T(4,128)}, f32[3,2048]{1,0:T(4,128)}) custom-call(f32[1,4,2,32,256]{4,3,2,1,0:T(8,128)S(1)} %get-tuple-element.8.res, f32[3,256]{1,0:T(4,128)S(1)} %get-tuple-element.9.pgrad, f32[8,8,128]{2,1,0:T(8,128)S(1)} %get-tuple-element.10.grads, s32[1,2048]{1,0:T(1,128)S(1)} %get-tuple-element.11.patch, ...), custom_call_target="tpu_custom_call" | custom-call | tf_op jit(solution)/shard_map/pallas_call | solution.py:447

commit v3 on v2

--- a/solution.py
+++ b/solution.py
@@ -38,7 +38,7 @@
     before_a, before_v, after_a, after_v,
     pick_row, pick_patch_t, normal8, morph_hi, morph_lo,
     dense, got, grads,
-    above_in, row_in, load, halo_send, halo_recv, send1, recv1, send3, recv3, morph_send, morph_recv,
+    row_in, all_in, load, halo_send, halo_recv, send1, recv1, send3, recv3, morph_send, morph_recv,
 ):
     _, fields, layers, ny, nz = adj.shape
     nodes = cell.shape[1]
@@ -56,6 +56,7 @@
         return lax.rem(y0 + d, n_yaw)
 
     has_before, has_after = s0 > 0, s0 < n_space - 1
+    last = jnp.logical_not(has_after)
 
     barrier = pltpu.get_barrier_semaphore()
 
@@ -73,7 +74,9 @@
     ]
     for copy in loads[:2]:
         copy.start()
-    each(n_yaw, lambda d: pl.semaphore_signal(barrier, inc=1, device_id={"yaw": yaw_peer(d)}))
+    pl.when(last)(lambda: each(
+        n_yaw, lambda d: pl.semaphore_signal(barrier, inc=1, device_id={"yaw": yaw_peer(d)})
+    ))
     each(n_space, lambda slab: pl.when(slab > s0 + 1)(lambda: enter(slab)), 2)
     for copy in loads[2:]:
         copy.start()
@@ -97,7 +100,7 @@
     def _():
         own_morph.start()
 
-    pl.semaphore_wait(barrier, s0 + has_after.astype(jnp.int32) + n_yaw - 1)
+    pl.semaphore_wait(barrier, s0 + jnp.where(last, n_yaw - 1, 1))
 
     def halo(slot, src, dst, peer):
         return pltpu.make_async_remote_copy(
@@ -114,7 +117,7 @@
         halo(3, visc_in.at[0, 0], after_v, s0 - 1),
     )
 
-    @pl.when(has_before)
+    @pl.when(jnp.logical_and(has_before, core == 0))
     def _():
         for copy in down:
             copy.start()
@@ -127,13 +130,20 @@
         for copy in up:
             copy.start()
 
-    each(n_space - 2, lambda slab: pl.when(slab < s0 - 1)(
-        lambda: pl.semaphore_signal(above_in, inc=1, device_id={"space": slab})
-    ), 0)
+    @pl.when(core == 1)
+    def _():
+        for copy in down:
+            copy.start()
 
     @pl.when(gives_near)
     def _():
         near_morph.start()
+
+    @pl.when(last)
+    def _():
+        each(n_yaw, lambda d: pl.semaphore_signal(row_in, inc=1, device_id={"yaw": yaw_peer(d)}))
+        pl.semaphore_wait(row_in, n_yaw - 1)
+        each(n_space - 1, lambda slab: pl.semaphore_signal(all_in, inc=1, device_id={"space": slab}), 0)
 
     @pl.when(jnp.logical_not(has_before))
     def _():
@@ -206,15 +216,9 @@
 
     @pl.when(is_site)
     def _():
-        m_hi, m_lo = parts(morph[...])
+        m_hi, m_lo = parts(morph[...].T)
         morph_hi[...] = m_hi
         morph_lo[...] = m_lo
-
-    @pl.when(s0 < n_space - 2)
-    def _():
-        pl.semaphore_wait(above_in, n_space - 2 - s0)
-
-    each(n_yaw, lambda d: pl.semaphore_signal(row_in, inc=1, device_id={"yaw": yaw_peer(d)}))
 
     @pl.when(has_before)
     def _():
@@ -266,100 +270,92 @@
     def owner_of(d):
         return lax.rem(mine + d, n_space)
 
+    def slot(yaw, slab):
+        return lax.rem(y0 - yaw + n_yaw, n_yaw) * n_space + lax.rem(s0 - slab + n_space, n_space)
+
+    def wait_blocks(sem, start, count):
+        blocks = got.at[start:start + count, 0:used]
+        pltpu.make_async_copy(blocks, blocks, sem).wait()
+
     def to_site(q, d):
         owner = owner_of(d)
         odd = lax.rem(owner, 2)
         return pltpu.make_async_remote_copy(
-            src_ref=dense.at[owner, 0:used], dst_ref=got.at[y0, s0, 0:used],
-            send_sem=send1.at[q, d], recv_sem=recv1.at[y0, s0],
+            src_ref=dense.at[owner, 0:used],
+            dst_ref=got.at[slot(2 * q + odd, owner - odd + 1), 0:used],
+            send_sem=send1, recv_sem=recv1,
             device_id={"yaw": 2 * q + odd, "space": owner - odd + 1},
         )
 
-    def from_slab(yaw, slab):
-        return pltpu.make_async_remote_copy(
-            src_ref=dense.at[0, 0:used], dst_ref=got.at[yaw, slab, 0:used],
-            send_sem=send1.at[0, 0], recv_sem=recv1.at[yaw, slab], device_id={"yaw": yaw, "space": slab},
-        )
-
-    def sites(act):
-        for q in range(n_yaw // 2):
-            @pl.when(jnp.logical_not(jnp.logical_and(is_site, pair == q)))
-            def _():
-                act(to_site(q, 0))
-
-            each(n_space, lambda d: act(to_site(q, d)))
-
-    pl.semaphore_wait(row_in, n_yaw - 1)
-    sites(lambda copy: copy.start())
+    pl.when(has_after)(lambda: pl.semaphore_wait(all_in, 1))
+    for q in range(n_yaw // 2):
+        @pl.when(jnp.logical_not(jnp.logical_and(is_site, pair == q)))
+        def _():
+            to_site(q, 0).start()
+
+        each(n_space, lambda d: to_site(q, d).start())
 
     def to_slab(k, slab):
         return pltpu.make_async_remote_copy(
             src_ref=grads.at[mine, 0:used], dst_ref=grads.at[mine, 0:used],
-            send_sem=send3.at[k, slab], recv_sem=recv3.at[mine],
+            send_sem=send3, recv_sem=recv3,
             device_id={"yaw": 2 * pair + k, "space": slab},
         )
 
-    def slabs(act):
-        def one(slab):
-            for k in range(2):
-                @pl.when(jnp.logical_not(jnp.logical_and(slab == s0, turn == k)))
-                def _():
-                    act(to_slab(k, slab))
-
-        each(n_space, one, 0)
-
-    def from_owner(d):
-        owner = owner_of(d)
-        return pltpu.make_async_remote_copy(
-            src_ref=grads.at[owner, 0:used], dst_ref=grads.at[owner, 0:used],
-            send_sem=send3.at[0, 0], recv_sem=recv3.at[owner],
-            device_id={"yaw": 2 * pair + lax.rem(owner, 2), "space": owner - lax.rem(owner, 2) + 1},
-        )
+    def to_slabs(slab):
+        for k in range(2):
+            @pl.when(jnp.logical_not(jnp.logical_and(slab == s0, turn == k)))
+            def _():
+                to_slab(k, slab).start()
 
     @pl.when(is_site)
     def _():
-        got[y0, s0] = dense[mine]
-        for dy in reversed(range(n_yaw)):
-            each(n_space, lambda d: from_slab(yaw_peer(dy), space_peer(d)).wait_recv(), 0 if dy else 1)
-        p = jnp.sum(jnp.sum(got[...], axis=0), axis=0)
+        got[0] = dense[mine]
+        wait_blocks(recv1, 1, n_yaw * n_space - 1)
+        p = jnp.sum(got[...], axis=0)
         p = jnp.concatenate([p[3 * h:3 * h + 3] for h in range(halves)], axis=1)
         p = jnp.concatenate([p, jnp.zeros((5, owned), F32)], axis=0)
         hi, lo = parts(p)
         both = jnp.concatenate([hi.astype(F32), lo.astype(F32)], axis=0).astype(BF16)
-        smooth = dot(both, morph_hi[...], ((1,), (1,))) + dot(both, morph_lo[...], ((1,), (1,)))
+        smooth = dot(both, morph_hi[...]) + dot(both, morph_lo[...])
         g = p + smooth[0:8] + smooth[8:16]
         for h in range(halves):
             grads[mine, 3 * h:3 * h + 3] = g[0:3, h * LANES:(h + 1) * LANES]
-        slabs(lambda copy: copy.start())
+        each(n_space, to_slabs, 0)
+
+    @pl.when(has_before)
+    def _():
+        for copy in down:
+            copy.wait_send()
+
+    @pl.when(has_after)
+    def _():
+        for copy in up:
+            copy.wait_send()
+
+    @pl.when(gives_near)
+    def _():
+        near_morph.wait_send()
+
+    sent = n_yaw // 2 * n_space
+
+    @pl.when(is_site)
+    def _():
+        wait_blocks(send1, 0, sent - 1)
+        wait_blocks(recv3, 0, n_space - 1)
 
     @pl.when(jnp.logical_not(is_site))
     def _():
-        from_owner(0).wait_recv()
-
-    each(n_space, lambda d: from_owner(d).wait_recv())
+        wait_blocks(send1, 0, sent)
+        wait_blocks(recv3, 0, n_space)
+
     for h in range(halves):
         pgrad[:, h * LANES:(h + 1) * LANES] = grads[s0, 3 * h:3 * h + 3]
     grads_out[...] = grads[...]
 
-    @pl.when(has_before)
-    def _():
-        for copy in down:
-            copy.wait_send()
-
-    @pl.when(has_after)
-    def _():
-        for copy in up:
-            copy.wait_send()
-
-    @pl.when(gives_near)
-    def _():
-        near_morph.wait_send()
-
-    sites(lambda copy: copy.wait_send())
-
     @pl.when(is_site)
     def _():
-        slabs(lambda copy: copy.wait_send())
+        wait_blocks(send3, 0, 2 * n_space - 1)
 
 
 def finish(res, pgrad, grads, patch, pick_patch, res_out, pgrad_out, ngrad_out, ngrad, sem):
@@ -429,12 +425,11 @@
             pltpu.VMEM((owned, owned), BF16),
             pltpu.VMEM((owned, owned), BF16),
             pltpu.VMEM((n_space, rows, LANES), F32),
-            pltpu.VMEM((n_yaw, n_space, rows, LANES), F32),
+            pltpu.VMEM((n_yaw * n_space, rows, LANES), F32),
             pltpu.VMEM((n_space, rows, LANES), F32),
             pltpu.SemaphoreType.REGULAR, pltpu.SemaphoreType.REGULAR,
             dma((8,)), dma((4,)), dma((4,)),
-            dma((n_yaw // 2, n_space)), dma((n_yaw, n_space)),
-            dma((2, n_space)), dma((n_space,)), dma, dma,
+            dma, dma, dma, dma, dma, dma,
         ],
         compiler_params=pltpu.CompilerParams(
             collective_id=0, has_side_effects=True, vmem_limit_bytes=56 * 1024 * 1024

time: 20 us -> 18.6 us (0.930)
  Pallas kernels: 18.5 us -> 17.2 us
    pallas_call x1, Pallas kernels: 17.6 us -> 16.2 us  [shards(): pl.pallas_call(functools.partial(kernel, n_yaw, n_space), out_shape=(pltp...]
where the time goes in v3:
time: 18.6 us; the launch traced here: 18.5 us
  Pallas kernels  17.2 us (92%)
  between operations  1.29 us (7%)
    pallas_call x1, Pallas kernels, shards(): pl.pallas_call(functools.partial(kernel, n_yaw, n_space), out_shape=(pltp...  16.2 us
    pallas_call x1, Pallas kernels, shards(): pl.pallas_call(finish, out_shape=(jax.ShapeDtypeStruct(adjoint.shape, F32...  0.95 us

profile of v3, /device:TPU:0, one launch (start us, length us, event | category | flops | bytes accessed | tf_op | source)
XLA Modules:
  0.0 18.5 jit_solution(427831951595587380)
XLA Ops:
  1.3 16.2 %shard_map.103 = (f32[1,4,2,32,256]{4,3,2,1,0:T(8,128)S(1)}, f32[3,256]{1,0:T(4,128)S(1)}, f32[8,8,128]{2,1,0:T(8,128)S(1)}, s32[1,2048]{1,0:T(1,128)S(1)}, bf16[256,2048]{1,0:T(8,128)(2,1)S(1)}) custom-call(f32[1,4,4]{2,1,0:T(4,128)} %coup_in.1, f32[1]{0:T(128)S(6)} %copy.11.weight_in, f32[1,4,2,32,256]{4,3,2,1,0:T(8,128)} %adj_in.1, ...), custom_call_target="tpu_custom_call" | custom-call | flops 400000000 | bytes 1000000 | tf_op jit(solution)/shard_map/pallas_call | solution.py:399
  17.5 0.9 %shard_map.104 = (f32[1,4,2,32,256]{4,3,2,1,0:T(8,128)}, f32[3,256]{1,0:T(4,128)}, f32[3,2048]{1,0:T(4,128)}) custom-call(f32[1,4,2,32,256]{4,3,2,1,0:T(8,128)S(1)} %get-tuple-element.8.res, f32[3,256]{1,0:T(4,128)S(1)} %get-tuple-element.9.pgrad, f32[8,8,128]{2,1,0:T(8,128)S(1)} %get-tuple-element.10.grads, s32[1,2048]{1,0:T(1,128)S(1)} %get-tuple-element.11.patch, ...), custom_call_target="tpu_custom_call" | custom-call | tf_op jit(solution)/shard_map/pallas_call | solution.py:442

commit v4 on v3

--- a/solution.py
+++ b/solution.py
@@ -9,6 +9,7 @@
 
 LANES = 128
 CHUNK = 256
+WIDE = 1024
 F32 = jnp.float32
 BF16 = jnp.bfloat16
 
@@ -37,7 +38,7 @@
     coup, weight, adj, visc, cell, normal, morph,
     before_a, before_v, after_a, after_v,
     pick_row, pick_patch_t, normal8, morph_hi, morph_lo,
-    dense, got, grads,
+    inner_sens, dense, got, grads,
     row_in, all_in, load, halo_send, halo_recv, send1, recv1, send3, recv3, morph_send, morph_recv,
 ):
     _, fields, layers, ny, nz = adj.shape
@@ -177,6 +178,7 @@
                 inner[nb] = 0.5 * (v + visc[0, nb])
                 total = total + inner[nb]
         total = total + 2.0
+        acc = jnp.zeros_like(v)
         for f in range(fields):
             a = adj[0, f, x]
             out = total * a
@@ -187,6 +189,8 @@
             for nb, face in inner.items():
                 out = out - face * adj[0, f, nb]
             res[0, f, x] = out
+            acc = acc + a * out
+        inner_sens[x] = acc
 
     cells = layers * ny
     for j in range(nodes // CHUNK):
@@ -230,38 +234,41 @@
         for copy in down:
             copy.wait_recv()
 
+    def outer(x):
+        return [(before_a, before_v)] * (x == 0) + [(after_a, after_v)] * (x == layers - 1)
+
     cell_sens = []
     for x in range(layers):
         v = visc[0, x]
-        acc = jnp.zeros_like(v)
-        for f in range(fields):
-            a = adj[0, f, x]
-            r = res[0, f, x]
-            if x == 0:
-                r = r - 0.5 * (v + before_v[...]) * (before_a[f] - a)
-            if x == layers - 1:
-                r = r - 0.5 * (v + after_v[...]) * (after_a[f] - a)
-            res[0, f, x] = r
-            acc = acc + a * r
+        acc = inner_sens[x]
+        for far_a, far_v in outer(x):
+            across = jnp.zeros_like(v)
+            for f in range(fields):
+                a = adj[0, f, x]
+                across = across + a * (far_a[f] - a)
+            acc = acc - 0.5 * (v + far_v[...]) * across
         cell_sens.append(weight[0] * v * acc)
     s = jnp.concatenate(cell_sens, axis=0)
     s = jnp.concatenate([s[:, g * LANES:(g + 1) * LANES] for g in range(groups)], axis=0)
     s = jnp.concatenate(parts(s.T), axis=1)
 
     owner_rows = n_space * rows
-    shape3 = (n_space, rows, CHUNK)
+    wide = WIDE if nodes % WIDE == 0 else CHUNK
+    shape3 = (n_space, rows, wide)
     half_of = lax.broadcasted_iota(jnp.int32, shape3, 0) * halves + lax.broadcasted_iota(jnp.int32, shape3, 1) // 3
     sums_now = jnp.zeros((2 * owner_rows, LANES), F32)
-    for j in range(nodes // CHUNK):
-        at = pl.ds(j * CHUNK, CHUNK)
+    for j in range(nodes // wide):
+        at = pl.ds(j * wide, wide)
         t = dot(s, pick_row[:, at])
         lane = cell[:, at] % LANES
         here = lax.broadcasted_iota(jnp.int32, t.shape, 0) == lane
         sens = jnp.sum(jnp.where(here, t, 0.0), axis=0, keepdims=True)
         part = normal8[:, at] * sens
-        high = patch[:, at] // LANES
-        spread = jnp.where(half_of == high[None], part[None], 0.0).reshape(owner_rows, CHUNK)
-        a = jnp.concatenate(parts(spread), axis=0)
+        hi = part.astype(BF16).astype(F32)
+        chosen = half_of == (patch[:, at] // LANES)[None]
+        a = jnp.concatenate([
+            jnp.where(chosen, piece[None], 0.0).reshape(owner_rows, wide).astype(BF16) for piece in (hi, part - hi)
+        ], axis=0)
         sums_now = sums_now + dot(a, pick_patch_t[at, :])
     dense[...] = (sums_now[:owner_rows] + sums_now[owner_rows:]).reshape(dense.shape)
 
@@ -294,6 +301,13 @@
             to_site(q, 0).start()
 
         each(n_space, lambda d: to_site(q, d).start())
+
+    for x in range(layers):
+        v = visc[0, x]
+        for far_a, far_v in outer(x):
+            face = 0.5 * (v + far_v[...])
+            for f in range(fields):
+                res[0, f, x] = res[0, f, x] - face * (far_a[f] - adj[0, f, x])
 
     def to_slab(k, slab):
         return pltpu.make_async_remote_copy(
@@ -424,6 +438,7 @@
             pltpu.VMEM((rows, nodes), F32),
             pltpu.VMEM((owned, owned), BF16),
             pltpu.VMEM((owned, owned), BF16),
+            pltpu.VMEM((layers, ny, nz), F32),
             pltpu.VMEM((n_space, rows, LANES), F32),
             pltpu.VMEM((n_yaw * n_space, rows, LANES), F32),
             pltpu.VMEM((n_space, rows, LANES), F32),

time: 18.6 us -> 18.5 us (level)
  Pallas kernels: 17.2 us -> 17 us
where the time goes in v4:
time: 18.5 us; the launch traced here: 18.3 us
  Pallas kernels  17 us (92%)
  between operations  1.29 us (7%)
    pallas_call x1, Pallas kernels, shards(): pl.pallas_call(functools.partial(kernel, n_yaw, n_space), out_shape=(pltp...  16.1 us
    pallas_call x1, Pallas kernels, shards(): pl.pallas_call(finish, out_shape=(jax.ShapeDtypeStruct(adjoint.shape, F32...  0.95 us

profile of v4, /device:TPU:0, one launch (start us, length us, event | category | flops | bytes accessed | tf_op | source)
XLA Modules:
  0.0 18.3 jit_solution(7279770602121355611)
XLA Ops:
  1.3 16.1 %shard_map.103 = (f32[1,4,2,32,256]{4,3,2,1,0:T(8,128)S(1)}, f32[3,256]{1,0:T(4,128)S(1)}, f32[8,8,128]{2,1,0:T(8,128)S(1)}, s32[1,2048]{1,0:T(1,128)S(1)}, bf16[256,2048]{1,0:T(8,128)(2,1)S(1)}) custom-call(f32[1,4,4]{2,1,0:T(4,128)} %coup_in.1, f32[1]{0:T(128)S(6)} %copy.11.weight_in, f32[1,4,2,32,256]{4,3,2,1,0:T(8,128)} %adj_in.1, ...), custom_call_target="tpu_custom_call" | custom-call | flops 400000000 | bytes 1000000 | tf_op jit(solution)/shard_map/pallas_call | solution.py:413
  17.4 0.9 %shard_map.104 = (f32[1,4,2,32,256]{4,3,2,1,0:T(8,128)}, f32[3,256]{1,0:T(4,128)}, f32[3,2048]{1,0:T(4,128)}) custom-call(f32[1,4,2,32,256]{4,3,2,1,0:T(8,128)S(1)} %get-tuple-element.8.res, f32[3,256]{1,0:T(4,128)S(1)} %get-tuple-element.9.pgrad, f32[8,8,128]{2,1,0:T(8,128)S(1)} %get-tuple-element.10.grads, s32[1,2048]{1,0:T(1,128)S(1)} %get-tuple-element.11.patch, ...), custom_call_target="tpu_custom_call" | custom-call | tf_op jit(solution)/shard_map/pallas_call | solution.py:457

commit v5 on v4

--- a/solution.py
+++ b/solution.py
@@ -33,9 +33,9 @@
 
 def kernel(
     n_yaw, n_space,
-    coup_in, weight_in, adj_in, visc_in, cell_in, patch_in, normal_in, morph_in,
-    res, pgrad, grads_out, patch, pick_patch,
-    coup, weight, adj, visc, cell, normal, morph,
+    coup_in, weight_in, adj_in, visc_in, cell_in, patch_in, tile_in, normal_in, morph_in,
+    res, pgrad, grads_out, tile,
+    coup, weight, adj, visc, cell, patch, normal, morph,
     before_a, before_v, after_a, after_v,
     pick_row, pick_patch_t, normal8, morph_hi, morph_lo,
     inner_sens, dense, got, grads,
@@ -70,15 +70,12 @@
         pltpu.make_async_copy(src, dst, load.at[i])
         for i, (src, dst) in enumerate((
             (adj_in, adj), (visc_in, visc), (coup_in, coup), (cell_in, cell), (patch_in, patch),
-            (normal_in, normal), (weight_in, weight),
+            (normal_in, normal), (weight_in, weight), (tile_in, tile),
         ))
     ]
     for copy in loads[:2]:
         copy.start()
-    pl.when(last)(lambda: each(
-        n_yaw, lambda d: pl.semaphore_signal(barrier, inc=1, device_id={"yaw": yaw_peer(d)})
-    ))
-    each(n_space, lambda slab: pl.when(slab > s0 + 1)(lambda: enter(slab)), 2)
+    each(n_space - 1, lambda slab: pl.when(slab > s0 + 1)(lambda: enter(slab)), 2)
     for copy in loads[2:]:
         copy.start()
     grads[...] = jnp.zeros_like(grads)
@@ -88,7 +85,7 @@
     turn = lax.rem(y0, 2)
     mine = first + turn
     is_site = core == 1
-    own_morph = pltpu.make_async_copy(morph_in, morph, load.at[7])
+    own_morph = pltpu.make_async_copy(morph_in, morph, load.at[8])
     near_morph = pltpu.make_async_remote_copy(
         src_ref=morph_in, dst_ref=morph, send_sem=morph_send, recv_sem=morph_recv,
         device_id={"space": first + 1},
@@ -101,7 +98,20 @@
     def _():
         own_morph.start()
 
-    pl.semaphore_wait(barrier, s0 + jnp.where(last, n_yaw - 1, 1))
+    @pl.when(has_after)
+    def _():
+        pl.semaphore_wait(barrier, s0 + 1)
+
+    @pl.when(s0 == n_space - 2)
+    def _():
+        pl.semaphore_signal(row_in, inc=1, device_id={"space": n_space - 1})
+
+    @pl.when(last)
+    def _():
+        pl.semaphore_wait(row_in, 1)
+        each(n_yaw, lambda d: pl.semaphore_signal(barrier, inc=1, device_id={"yaw": yaw_peer(d)}))
+        pl.semaphore_wait(barrier, n_yaw)
+        each(n_space - 1, lambda slab: pl.semaphore_signal(all_in, inc=1, device_id={"space": slab}), 0)
 
     def halo(slot, src, dst, peer):
         return pltpu.make_async_remote_copy(
@@ -139,12 +149,6 @@
     @pl.when(gives_near)
     def _():
         near_morph.start()
-
-    @pl.when(last)
-    def _():
-        each(n_yaw, lambda d: pl.semaphore_signal(row_in, inc=1, device_id={"yaw": yaw_peer(d)}))
-        pl.semaphore_wait(row_in, n_yaw - 1)
-        each(n_space - 1, lambda slab: pl.semaphore_signal(all_in, inc=1, device_id={"space": slab}), 0)
 
     @pl.when(jnp.logical_not(has_before))
     def _():
@@ -204,8 +208,6 @@
         low = patch[:, at] % LANES
         hot = (lax.broadcasted_iota(jnp.int32, (LANES, CHUNK), 0) == low).astype(F32)
         pick_patch_t[at, :] = hot.T.astype(BF16)
-        pick_patch[0:LANES, at] = hot.astype(BF16)
-        pick_patch[LANES:2 * LANES, at] = hot.astype(BF16)
     normal8[...] = jnp.zeros_like(normal8)
     for h in range(halves):
         normal8[3 * h:3 * h + 3, :] = normal[...]
@@ -274,9 +276,6 @@
 
     pair = lax.div(y0, 2)
 
-    def owner_of(d):
-        return lax.rem(mine + d, n_space)
-
     def slot(yaw, slab):
         return lax.rem(y0 - yaw + n_yaw, n_yaw) * n_space + lax.rem(s0 - slab + n_space, n_space)
 
@@ -284,8 +283,7 @@
         blocks = got.at[start:start + count, 0:used]
         pltpu.make_async_copy(blocks, blocks, sem).wait()
 
-    def to_site(q, d):
-        owner = owner_of(d)
+    def to_site(q, owner):
         odd = lax.rem(owner, 2)
         return pltpu.make_async_remote_copy(
             src_ref=dense.at[owner, 0:used],
@@ -295,12 +293,15 @@
         )
 
     pl.when(has_after)(lambda: pl.semaphore_wait(all_in, 1))
+    def to_sites(q, i):
+        owner = n_space - 1 - i
+
+        @pl.when(jnp.logical_not(jnp.logical_and(is_site, jnp.logical_and(pair == q, owner == mine))))
+        def _():
+            to_site(q, owner).start()
+
     for q in range(n_yaw // 2):
-        @pl.when(jnp.logical_not(jnp.logical_and(is_site, pair == q)))
-        def _():
-            to_site(q, 0).start()
-
-        each(n_space, lambda d: to_site(q, d).start())
+        each(n_space, functools.partial(to_sites, q), 0)
 
     for x in range(layers):
         v = visc[0, x]
@@ -372,9 +373,8 @@
         wait_blocks(send3, 0, 2 * n_space - 1)
 
 
-def finish(res, pgrad, grads, patch, pick_patch, res_out, pgrad_out, ngrad_out, ngrad, sem):
-    n_space, rows, _ = grads.shape
-    nodes = patch.shape[1]
+def finish(res, pgrad, grads, tile, res_out, pgrad_out, ngrad_out, ngrad, sem):
+    n_space = grads.shape[0]
     halves = pgrad.shape[1] // LANES
     copies = [
         pltpu.make_async_copy(src, dst, sem.at[i])
@@ -382,18 +382,21 @@
     ]
     for copy in copies[:2]:
         copy.start()
-    shape3 = (n_space, rows, CHUNK)
-    half_of = lax.broadcasted_iota(jnp.int32, shape3, 0) * halves + lax.broadcasted_iota(jnp.int32, shape3, 1) // 3
-    allg = jnp.concatenate(parts(grads[...].reshape(n_space * rows, LANES)), axis=1)
-    for j in range(nodes // CHUNK):
-        at = pl.ds(j * CHUNK, CHUNK)
-        e = dot(allg, pick_patch[:, at]).reshape(shape3)
-        high = patch[:, at] // LANES
-        e = jnp.sum(jnp.where(half_of == high[None], e, 0.0), axis=0)
-        out = e[0:3]
-        for h in range(1, halves):
-            out = out + e[3 * h:3 * h + 3]
-        ngrad[:, at] = out
+    for block in range(tile.shape[0] // 8):
+        node_patch = tile[8 * block:8 * block + 8]
+        low, high = node_patch % LANES, node_patch // LANES
+        out = [jnp.zeros(low.shape, F32)] * 3
+        for owner in range(n_space):
+            for h in range(halves):
+                here = high == owner * halves + h
+                for c in range(3):
+                    row = jnp.broadcast_to(grads[owner, 3 * h + c:3 * h + c + 1], low.shape)
+                    value = jnp.take_along_axis(row, low, axis=1, mode="promise_in_bounds")
+                    out[c] = jnp.where(here, value, out[c])
+        for c in range(3):
+            for r in range(8):
+                at = (8 * block + r) * LANES
+                ngrad[c:c + 1, at:at + LANES] = out[c][r:r + 1]
     copies[2].start()
     for copy in copies:
         copy.wait()
@@ -416,16 +419,16 @@
             pltpu.VMEM(adjoint.shape, F32),
             pltpu.VMEM((3, owned), F32),
             pltpu.VMEM((n_space, rows, LANES), F32),
-            pltpu.VMEM((1, nodes), jnp.int32),
-            pltpu.VMEM((2 * LANES, nodes), BF16),
+            pltpu.VMEM((nodes // LANES, LANES), jnp.int32),
         ),
-        in_specs=[pl.BlockSpec(memory_space=pltpu.HBM)] * 8,
-        out_specs=(vmem,) * 5,
+        in_specs=[pl.BlockSpec(memory_space=pltpu.HBM)] * 9,
+        out_specs=(vmem,) * 4,
         scratch_shapes=[
             pltpu.SMEM(coupling.shape, F32),
             pltpu.SMEM((1,), F32),
             pltpu.VMEM(adjoint.shape, F32),
             pltpu.VMEM(viscosity.shape, F32),
+            pltpu.VMEM((1, nodes), jnp.int32),
             pltpu.VMEM((1, nodes), jnp.int32),
             pltpu.VMEM(node_normal.shape, F32),
             pltpu.VMEM(morph_kernel.shape, F32),
@@ -443,7 +446,7 @@
             pltpu.VMEM((n_yaw * n_space, rows, LANES), F32),
             pltpu.VMEM((n_space, rows, LANES), F32),
             pltpu.SemaphoreType.REGULAR, pltpu.SemaphoreType.REGULAR,
-            dma((8,)), dma((4,)), dma((4,)),
+            dma((9,)), dma((4,)), dma((4,)),
             dma, dma, dma, dma, dma, dma,
         ],
         compiler_params=pltpu.CompilerParams(
@@ -452,7 +455,7 @@
         cost_estimate=pl.CostEstimate(flops=400_000_000, bytes_accessed=1_000_000, transcendentals=0),
     )(
         coupling, yaw_weight, adjoint, viscosity,
-        node_cell[None], node_patch[None], node_normal, morph_kernel,
+        node_cell[None], node_patch[None], node_patch.reshape(nodes // LANES, LANES), node_normal, morph_kernel,
     )
     return pl.pallas_call(
         finish,
@@ -461,7 +464,7 @@
             jax.ShapeDtypeStruct((3, owned), F32),
             jax.ShapeDtypeStruct((3, nodes), F32),
         ),
-        in_specs=[vmem] * 5,
+        in_specs=[vmem] * 4,
         out_specs=(anywhere,) * 3,
         scratch_shapes=[pltpu.VMEM((3, nodes), F32), dma((3,))],
         compiler_params=pltpu.CompilerParams(vmem_limit_bytes=4 * 1024 * 1024),

time: 18.5 us -> 18.1 us (0.978)
  Pallas kernels: 17 us -> 16.7 us
    pallas_call x1, Pallas kernels: 16.1 us -> 15.8 us  [shards(): pl.pallas_call(functools.partial(kernel, n_yaw, n_space), out_shape=(pltp...]
where the time goes in v5:
time: 18.1 us; the launch traced here: 18 us
  Pallas kernels  16.7 us (92%)
  between operations  1.29 us (7%)
    pallas_call x1, Pallas kernels, shards(): pl.pallas_call(functools.partial(kernel, n_yaw, n_space), out_shape=(pltp...  15.8 us
    pallas_call x1, Pallas kernels, shards(): pl.pallas_call(finish, out_shape=(jax.ShapeDtypeStruct(adjoint.shape, F32...  0.83 us

profile of v5, /device:TPU:0, one launch (start us, length us, event | category | flops | bytes accessed | tf_op | source)
XLA Modules:
  0.0 18.0 jit_solution(16426273686978524864)
XLA Ops:
  1.3 15.8 %shard_map.103 = (f32[1,4,2,32,256]{4,3,2,1,0:T(8,128)S(1)}, f32[3,256]{1,0:T(4,128)S(1)}, f32[8,8,128]{2,1,0:T(8,128)S(1)}, s32[16,128]{1,0:T(8,128)S(1)}) custom-call(f32[1,4,4]{2,1,0:T(4,128)} %coup_in.1, f32[1]{0:T(128)S(6)} %copy.11.weight_in, f32[1,4,2,32,256]{4,3,2,1,0:T(8,128)} %adj_in.1, f32[1,2,32,256]{3,2,1,0:T(8,128)} %visc_in.1, ...), custom_call_target="tpu_custom_call" | custom-call | flops 400000000 | bytes 1000000 | tf_op jit(solution)/shard_map/pallas_call | solution.py:416
  17.1 0.8 %shard_map.104 = (f32[1,4,2,32,256]{4,3,2,1,0:T(8,128)}, f32[3,256]{1,0:T(4,128)}, f32[3,2048]{1,0:T(4,128)}) custom-call(f32[1,4,2,32,256]{4,3,2,1,0:T(8,128)S(1)} %get-tuple-element.7.res, f32[3,256]{1,0:T(4,128)S(1)} %get-tuple-element.8.pgrad, f32[8,8,128]{2,1,0:T(8,128)S(1)} %get-tuple-element.9.grads, s32[16,128]{1,0:T(8,128)S(1)} %get-tuple-element.10.tile), custom_call_target="tpu_custom_call" | custom-call | tf_op jit(solution)/shard_map/pallas_call | solution.py:460

commit v6 on v5

--- a/solution.py
+++ b/solution.py
@@ -9,7 +9,6 @@
 
 LANES = 128
 CHUNK = 256
-WIDE = 1024
 F32 = jnp.float32
 BF16 = jnp.bfloat16
 
@@ -36,13 +35,13 @@
     coup_in, weight_in, adj_in, visc_in, cell_in, patch_in, tile_in, normal_in, morph_in,
     res, pgrad, grads_out, tile,
     coup, weight, adj, visc, cell, patch, normal, morph,
-    before_a, before_v, after_a, after_v,
-    pick_row, pick_patch_t, normal8, morph_hi, morph_lo,
+    far_a, far_v,
+    cell_sens, near_sens, pick_patch_t, normal8, morph_hi, morph_lo,
     inner_sens, dense, got, grads,
     row_in, all_in, load, halo_send, halo_recv, send1, recv1, send3, recv3, morph_send, morph_recv,
 ):
     _, fields, layers, ny, nz = adj.shape
-    nodes = cell.shape[1]
+    nodes = patch.shape[1]
     owned = morph.shape[1]
     halves = owned // LANES
     used = 3 * halves
@@ -120,12 +119,12 @@
         )
 
     up = (
-        halo(0, adj.at[0, :, layers - 1], before_a, s0 + 1),
-        halo(1, visc.at[0, layers - 1], before_v, s0 + 1),
+        halo(0, adj.at[0, :, layers - 1], far_a.at[0], s0 + 1),
+        halo(1, visc.at[0, layers - 1], far_v.at[0], s0 + 1),
     )
     down = (
-        halo(2, adj_in.at[0, :, 0], after_a, s0 - 1),
-        halo(3, visc_in.at[0, 0], after_v, s0 - 1),
+        halo(2, adj_in.at[0, :, 0], far_a.at[1], s0 - 1),
+        halo(3, visc_in.at[0, 0], far_v.at[1], s0 - 1),
     )
 
     @pl.when(jnp.logical_and(has_before, core == 0))
@@ -152,13 +151,13 @@
 
     @pl.when(jnp.logical_not(has_before))
     def _():
-        before_a[...] = jnp.zeros_like(before_a)
-        before_v[...] = jnp.zeros_like(before_v)
+        far_a[0] = jnp.zeros_like(far_a[0])
+        far_v[0] = jnp.zeros_like(far_v[0])
 
     @pl.when(jnp.logical_not(has_after))
     def _():
-        after_a[...] = jnp.zeros_like(after_a)
-        after_v[...] = jnp.zeros_like(after_v)
+        far_a[1] = jnp.zeros_like(far_a[1])
+        far_v[1] = jnp.zeros_like(far_v[1])
 
     for copy in loads[2:]:
         copy.wait()
@@ -196,15 +195,8 @@
             acc = acc + a * out
         inner_sens[x] = acc
 
-    cells = layers * ny
     for j in range(nodes // CHUNK):
         at = pl.ds(j * CHUNK, CHUNK)
-        c = cell[:, at]
-        row = (c // LANES) % groups * cells + c // nz
-        count = groups * cells
-        hot = (lax.broadcasted_iota(jnp.int32, (count, CHUNK), 0) == row).astype(F32).astype(BF16)
-        pick_row[0:count, at] = hot
-        pick_row[count:2 * count, at] = hot
         low = patch[:, at] % LANES
         hot = (lax.broadcasted_iota(jnp.int32, (LANES, CHUNK), 0) == low).astype(F32)
         pick_patch_t[at, :] = hot.T.astype(BF16)
@@ -226,46 +218,63 @@
         morph_hi[...] = m_hi
         morph_lo[...] = m_lo
 
-    @pl.when(has_before)
+    def sens_of(side):
+        x = side * (layers - 1)
+        v = visc[0, x]
+        across = jnp.zeros_like(v)
+        for f in range(fields):
+            a = adj[0, f, x]
+            across = across + a * (far_a[side, f] - a)
+        acc = inner_sens[x] - 0.5 * (v + far_v[side]) * across
+        cell_sens[side] = weight[0] * v * acc
+
+    def at_nodes(side, block):
+        here = cell[8 * block:8 * block + 8]
+        lane, row = here % LANES, here // LANES - side * ((layers - 1) * ny * groups)
+        found = [jnp.zeros(lane.shape, F32)] * groups
+        for y in range(ny):
+            for g in range(groups):
+                source = jnp.broadcast_to(cell_sens[side, y:y + 1, g * LANES:(g + 1) * LANES], lane.shape)
+                value = jnp.take_along_axis(source, lane, axis=1, mode="promise_in_bounds")
+                found[g] = jnp.where(row == y * groups + g, value, found[g])
+        return sum(found[1:], found[0])
+
+    @pl.when(jnp.logical_and(core == 0, has_after))
+    def _():
+        for copy in down:
+            copy.wait_recv()
+
+    @pl.when(core == 1)
     def _():
         for copy in up:
             copy.wait_recv()
 
-    @pl.when(has_after)
+    sens_of(1 - core)
+    for block in range(nodes // (8 * LANES)):
+        near_sens[8 * block:8 * block + 8] = at_nodes(1 - core, block)
+
+    @pl.when(jnp.logical_and(core == 0, has_before))
+    def _():
+        for copy in up:
+            copy.wait_recv()
+
+    @pl.when(jnp.logical_and(core == 1, has_after))
     def _():
         for copy in down:
             copy.wait_recv()
 
-    def outer(x):
-        return [(before_a, before_v)] * (x == 0) + [(after_a, after_v)] * (x == layers - 1)
-
-    cell_sens = []
-    for x in range(layers):
-        v = visc[0, x]
-        acc = inner_sens[x]
-        for far_a, far_v in outer(x):
-            across = jnp.zeros_like(v)
-            for f in range(fields):
-                a = adj[0, f, x]
-                across = across + a * (far_a[f] - a)
-            acc = acc - 0.5 * (v + far_v[...]) * across
-        cell_sens.append(weight[0] * v * acc)
-    s = jnp.concatenate(cell_sens, axis=0)
-    s = jnp.concatenate([s[:, g * LANES:(g + 1) * LANES] for g in range(groups)], axis=0)
-    s = jnp.concatenate(parts(s.T), axis=1)
-
+    sens_of(core)
     owner_rows = n_space * rows
-    wide = WIDE if nodes % WIDE == 0 else CHUNK
+    wide = 8 * LANES
     shape3 = (n_space, rows, wide)
     half_of = lax.broadcasted_iota(jnp.int32, shape3, 0) * halves + lax.broadcasted_iota(jnp.int32, shape3, 1) // 3
     sums_now = jnp.zeros((2 * owner_rows, LANES), F32)
     for j in range(nodes // wide):
         at = pl.ds(j * wide, wide)
-        t = dot(s, pick_row[:, at])
-        lane = cell[:, at] % LANES
-        here = lax.broadcasted_iota(jnp.int32, t.shape, 0) == lane
-        sens = jnp.sum(jnp.where(here, t, 0.0), axis=0, keepdims=True)
-        part = normal8[:, at] * sens
+        sens = near_sens[8 * j:8 * j + 8] + at_nodes(core, j)
+        part = jnp.concatenate([
+            normal8[:, j * wide + r * LANES:j * wide + (r + 1) * LANES] * sens[r:r + 1] for r in range(8)
+        ], axis=1)
         hi = part.astype(BF16).astype(F32)
         chosen = half_of == (patch[:, at] // LANES)[None]
         a = jnp.concatenate([
@@ -303,12 +312,11 @@
     for q in range(n_yaw // 2):
         each(n_space, functools.partial(to_sites, q), 0)
 
-    for x in range(layers):
-        v = visc[0, x]
-        for far_a, far_v in outer(x):
-            face = 0.5 * (v + far_v[...])
-            for f in range(fields):
-                res[0, f, x] = res[0, f, x] - face * (far_a[f] - adj[0, f, x])
+    for side in range(2):
+        x = side * (layers - 1)
+        face = 0.5 * (visc[0, x] + far_v[side])
+        for f in range(fields):
+            res[0, f, x] = res[0, f, x] - face * (far_a[side, f] - adj[0, f, x])
 
     def to_slab(k, slab):
         return pltpu.make_async_remote_copy(
@@ -428,15 +436,14 @@
             pltpu.SMEM((1,), F32),
             pltpu.VMEM(adjoint.shape, F32),
             pltpu.VMEM(viscosity.shape, F32),
-            pltpu.VMEM((1, nodes), jnp.int32),
+            pltpu.VMEM((nodes // LANES, LANES), jnp.int32),
             pltpu.VMEM((1, nodes), jnp.int32),
             pltpu.VMEM(node_normal.shape, F32),
             pltpu.VMEM(morph_kernel.shape, F32),
-            pltpu.VMEM((fields, ny, nz), F32),
-            pltpu.VMEM((ny, nz), F32),
-            pltpu.VMEM((fields, ny, nz), F32),
-            pltpu.VMEM((ny, nz), F32),
-            pltpu.VMEM((2 * layers * ny * nz // LANES, nodes), BF16),
+            pltpu.VMEM((2, fields, ny, nz), F32),
+            pltpu.VMEM((2, ny, nz), F32),
+            pltpu.VMEM((2, ny, nz), F32),
+            pltpu.VMEM((nodes // LANES, LANES), F32),
             pltpu.VMEM((nodes, LANES), BF16),
             pltpu.VMEM((rows, nodes), F32),
             pltpu.VMEM((owned, owned), BF16),
@@ -455,7 +462,7 @@
         cost_estimate=pl.CostEstimate(flops=400_000_000, bytes_accessed=1_000_000, transcendentals=0),
     )(
         coupling, yaw_weight, adjoint, viscosity,
-        node_cell[None], node_patch[None], node_patch.reshape(nodes // LANES, LANES), node_normal, morph_kernel,
+        node_cell.reshape(nodes // LANES, LANES), node_patch[None], node_patch.reshape(nodes // LANES, LANES), node_normal, morph_kernel,
     )
     return pl.pallas_call(
         finish,

time: 18.1 us -> 17.9 us (0.989)
  Pallas kernels: 16.7 us -> 16.5 us
where the time goes in v6:
time: 17.9 us; the launch traced here: 17.8 us
  Pallas kernels  16.5 us (92%)
  between operations  1.29 us (7%)
    pallas_call x1, Pallas kernels, shards(): pl.pallas_call(functools.partial(kernel, n_yaw, n_space), out_shape=(pltp...  15.7 us
    pallas_call x1, Pallas kernels, shards(): pl.pallas_call(finish, out_shape=(jax.ShapeDtypeStruct(adjoint.shape, F32...  0.83 us

profile of v6, /device:TPU:0, one launch (start us, length us, event | category | flops | bytes accessed | tf_op | source)
XLA Modules:
  0.0 17.8 jit_solution(4752274049696096023)
XLA Ops:
  1.3 15.7 %shard_map.103 = (f32[1,4,2,32,256]{4,3,2,1,0:T(8,128)S(1)}, f32[3,256]{1,0:T(4,128)S(1)}, f32[8,8,128]{2,1,0:T(8,128)S(1)}, s32[16,128]{1,0:T(8,128)S(1)}) custom-call(f32[1,4,4]{2,1,0:T(4,128)} %coup_in.1, f32[1]{0:T(128)S(6)} %copy.11.weight_in, f32[1,4,2,32,256]{4,3,2,1,0:T(8,128)} %adj_in.1, f32[1,2,32,256]{3,2,1,0:T(8,128)} %visc_in.1, ...), custom_call_target="tpu_custom_call" | custom-call | flops 400000000 | bytes 1000000 | tf_op jit(solution)/shard_map/pallas_call | solution.py:424
  17.0 0.8 %shard_map.104 = (f32[1,4,2,32,256]{4,3,2,1,0:T(8,128)}, f32[3,256]{1,0:T(4,128)}, f32[3,2048]{1,0:T(4,128)}) custom-call(f32[1,4,2,32,256]{4,3,2,1,0:T(8,128)S(1)} %get-tuple-element.7.res, f32[3,256]{1,0:T(4,128)S(1)} %get-tuple-element.8.pgrad, f32[8,8,128]{2,1,0:T(8,128)S(1)} %get-tuple-element.9.grads, s32[16,128]{1,0:T(8,128)S(1)} %get-tuple-element.10.tile), custom_call_target="tpu_custom_call" | custom-call | tf_op jit(solution)/shard_map/pallas_call | solution.py:467

commit v7 on v6

--- a/solution.py
+++ b/solution.py
@@ -75,8 +75,6 @@
     for copy in loads[:2]:
         copy.start()
     each(n_space - 1, lambda slab: pl.when(slab > s0 + 1)(lambda: enter(slab)), 2)
-    for copy in loads[2:]:
-        copy.start()
     grads[...] = jnp.zeros_like(grads)
 
     core = lax.rem(s0, 2)
@@ -144,6 +142,9 @@
     def _():
         for copy in down:
             copy.start()
+
+    for copy in loads[2:]:
+        copy.start()
 
     @pl.when(gives_near)
     def _():

time: 17.9 us -> 18 us (level)
  no operation moved by 1% of the time
where the time goes in v7:
time: 18 us; the launch traced here: 17.8 us
  Pallas kernels  16.5 us (92%)
  between operations  1.29 us (7%)
    pallas_call x1, Pallas kernels, shards(): pl.pallas_call(functools.partial(kernel, n_yaw, n_space), out_shape=(pltp...  15.7 us
    pallas_call x1, Pallas kernels, shards(): pl.pallas_call(finish, out_shape=(jax.ShapeDtypeStruct(adjoint.shape, F32...  0.83 us

profile of v7, /device:TPU:0, one launch (start us, length us, event | category | flops | bytes accessed | tf_op | source)
XLA Modules:
  0.0 17.8 jit_solution(5989703694523030035)
XLA Ops:
  1.3 15.7 %shard_map.103 = (f32[1,4,2,32,256]{4,3,2,1,0:T(8,128)S(1)}, f32[3,256]{1,0:T(4,128)S(1)}, f32[8,8,128]{2,1,0:T(8,128)S(1)}, s32[16,128]{1,0:T(8,128)S(1)}) custom-call(f32[1,4,4]{2,1,0:T(4,128)} %coup_in.1, f32[1]{0:T(128)S(6)} %copy.11.weight_in, f32[1,4,2,32,256]{4,3,2,1,0:T(8,128)} %adj_in.1, f32[1,2,32,256]{3,2,1,0:T(8,128)} %visc_in.1, ...), custom_call_target="tpu_custom_call" | custom-call | flops 400000000 | bytes 1000000 | tf_op jit(solution)/shard_map/pallas_call | solution.py:425
  17.0 0.8 %shard_map.104 = (f32[1,4,2,32,256]{4,3,2,1,0:T(8,128)}, f32[3,256]{1,0:T(4,128)}, f32[3,2048]{1,0:T(4,128)}) custom-call(f32[1,4,2,32,256]{4,3,2,1,0:T(8,128)S(1)} %get-tuple-element.7.res, f32[3,256]{1,0:T(4,128)S(1)} %get-tuple-element.8.pgrad, f32[8,8,128]{2,1,0:T(8,128)S(1)} %get-tuple-element.9.grads, s32[16,128]{1,0:T(8,128)S(1)} %get-tuple-element.10.tile), custom_call_target="tpu_custom_call" | custom-call | tf_op jit(solution)/shard_map/pallas_call | solution.py:468
